TPU v7x, 32 devices: a whole 2x2x4 slice. The times are simulated.
32 devices in a mesh: seq: 4 (over y, x), mp: 8 (over z, core).
Axes of the slice: x: 2, y: 2, z: 4, core: 2. Of those that a mesh axis runs over, the one named last changes fastest.
Arguments:
- audio_feats: bfloat16 [16384, 512], P(('seq', 'mp')), may hold values from -6 to 6
- conv_first: bfloat16 [3, 3, 512, 256], replicated, may hold values from -0.15625 to 0.15625
- conv_second: bfloat16 [3, 256, 512], replicated, may hold values from -0.375 to 0.375
- down_weight: bfloat16 [16, 512, 512], replicated, may hold values from -0.09375 to 0.09375
- in_proj: bfloat16 [512, 4096], replicated, may hold values from -0.25 to 0.25
- norm_gain: float32 [4096], replicated, may hold values from 0.25 to 1.75
- qkv_weight: bfloat16 [3, 4096, 2048], P(None, None, 'mp'), may hold values from -0.09375 to 0.09375
- out_weight: bfloat16 [2048, 4096], P('mp'), may hold values from -0.125 to 0.125
Outputs:
- layer_out: bfloat16 [2048, 4096], P(('seq', 'mp'))
All inputs are finite; a program needn't handle non-finite values.
Results may differ from a plain program's by a relative error of at most 0.023.
Values may be sent and summed in bfloat16 or wider, within the bound.
A program may use at most 128 MiB of HBM per device.

v0:
```python
import jax
import jax.numpy as jnp
from jax import lax
from jax.sharding import PartitionSpec as P

HD = 128
STRIDE = 8


def from_behind(block, axis, distance):
    devices = range(lax.axis_size(axis))
    route = [(i - distance, i) for i in devices if i - distance in devices]
    return lax.ppermute(block, axis, route)


def unit_apply(extended, first, second, dilation):
    count = extended.shape[0] - 2 * dilation
    act = jax.nn.elu(extended.astype(jnp.float32)).astype(jnp.bfloat16)
    middle = jnp.dot(act[0:count], first[0], preferred_element_type=jnp.float32)
    middle = middle + jnp.dot(
        act[dilation : dilation + count], first[1], preferred_element_type=jnp.float32
    )
    middle = middle + jnp.dot(
        act[2 * dilation : 2 * dilation + count], first[2], preferred_element_type=jnp.float32
    )
    inner = jax.nn.elu(middle).astype(jnp.bfloat16)
    kept = extended[2 * dilation :].astype(jnp.float32)
    return (kept + jnp.dot(inner, second, preferred_element_type=jnp.float32)).astype(jnp.bfloat16)


def body(
    audio_feats, conv_first, conv_second, down_weight, in_proj, norm_gain, qkv_weight, out_weight
):
    dilations = (1, 3, 9)
    channels = audio_feats.shape[1]
    depth = 2 * sum(dilations) + STRIDE
    rows = audio_feats.shape[0]
    extended = jnp.concatenate(
        [from_behind(audio_feats[rows - depth :], ("seq", "mp"), 1), audio_feats], axis=0
    )
    for unit in range(3):
        extended = unit_apply(extended, conv_first[unit], conv_second[unit], dilations[unit])
    act = jax.nn.elu(extended.astype(jnp.float32)).astype(jnp.bfloat16)
    grouped = act.reshape(-1, STRIDE * channels)
    taps = down_weight.reshape(2, STRIDE * channels, channels)
    latent = (
        jnp.dot(grouped[:-1], taps[0], preferred_element_type=jnp.float32)
        + jnp.dot(grouped[1:], taps[1], preferred_element_type=jnp.float32)
    ).astype(jnp.bfloat16)
    frames_mine = jnp.dot(latent, in_proj, preferred_element_type=jnp.float32).astype(jnp.bfloat16)
    wide = lax.all_gather(frames_mine, "mp", axis=0, tiled=True).astype(jnp.float32)
    normed = (
        wide * lax.rsqrt(jnp.mean(wide * wide, axis=1, keepdims=True) + 1e-05) * norm_gain
    ).astype(jnp.bfloat16)
    outputs = [
        jnp.dot(normed, qkv_weight[index], preferred_element_type=jnp.float32).astype(jnp.bfloat16)
        for index in range(3)
    ]
    stacked = jnp.stack(outputs, axis=0)
    query, keys, values = (stacked[0], stacked[1], stacked[2])
    length = query.shape[0]
    columns = query.shape[1]
    local_heads = columns // HD
    heads_q = query.reshape(length, local_heads, HD)
    q_start = lax.axis_index("seq") * length
    qpos = q_start + jnp.arange(length, dtype=jnp.int32)
    scale = HD ** (-0.5)
    init = (
        jnp.full((local_heads, length), -1e30, jnp.float32),
        jnp.zeros((local_heads, length), jnp.float32),
        jnp.zeros((local_heads, length, HD), jnp.float32),
    )
    carry = init
    start = jnp.int32(0)
    key_piece = lax.all_gather(keys, "seq", axis=0, tiled=True)
    value_piece = lax.all_gather(values, "seq", axis=0, tiled=True)
    rows = key_piece.shape[0]
    nblock = max(1, rows // 1024)
    blen = rows // nblock
    for index in range(nblock):
        k_start = start + index * blen
        key_block = key_piece[index * blen : (index + 1) * blen].reshape(blen, local_heads, HD)
        value_block = value_piece[index * blen : (index + 1) * blen].reshape(blen, local_heads, HD)
        update_peak, update_total, update_accum = carry
        scores = (
            jnp.einsum("qhd,khd->hqk", heads_q, key_block, preferred_element_type=jnp.float32)
            * scale
        )
        kpos = k_start + jnp.arange(blen, dtype=jnp.int32)
        mask = (kpos[None, :] <= qpos[:, None])[None]
        scores = jnp.where(mask, scores, -1e30)
        fresh = jnp.maximum(update_peak, jnp.max(scores, axis=2))
        probs = jnp.where(mask, jnp.exp(scores - fresh[:, :, None]), 0.0)
        factor = jnp.exp(update_peak - fresh)
        update_total = update_total * factor + jnp.sum(probs, axis=2)
        mixed = jnp.einsum(
            "hqk,khd->hqd",
            probs.astype(jnp.bfloat16),
            value_block,
            preferred_element_type=jnp.float32,
        )
        carry = (fresh, update_total, update_accum * factor[:, :, None] + mixed)
    peak, total, accum = carry
    attn = (
        (accum / total[:, :, None]).transpose(1, 0, 2).reshape(length, columns).astype(jnp.bfloat16)
    )
    summed = lax.psum_scatter(
        jnp.dot(attn, out_weight, preferred_element_type=jnp.float32).astype(jnp.bfloat16),
        "mp",
        scatter_dimension=0,
        tiled=True,
    ).astype(jnp.float32)
    return (frames_mine.astype(jnp.float32) + summed).astype(jnp.bfloat16)


def solution(mesh):
    placed = (P(("seq", "mp"), None), P(), P(), P(), P(), P(), P(None, None, "mp"), P("mp", None))
    return jax.shard_map(
        body, mesh=mesh, in_specs=placed, out_specs=P(("seq", "mp"), None), check_vma=False
    )
```

profile of v0, /device:TPU:6, one launch (start us, length us, event | category | flops | bytes accessed | tf_op | source)
XLA Modules:
  0.0 228.5 jit_solution(2340841109663911952)
XLA Ops:
  6.5 0.0 copy-start
  6.5 0.0 all-gather.4.cloned.1.call-start
  6.5 0.9 slice.137
  7.5 0.0 copy-start.3
  7.5 2.1 collective-permute-start
  9.6 5.7 %fusion.145 = (bf16[8,512,512]{2,1,0:T(8,128)(2,1)}, bf16[8,512,512]{2,1,0:T(8,128)(2,1)}) fusion(bf16[16,512,512]{2,1,0:T(8,128)(2,1)} %param.11), kind=kLoop, calls=%fused_computation.157 | loop fusion | bytes 16777216 | tf_op jit(solution)/shard_map/slice | solution.py:48
  15.3 0.4 collective-permute-done
  15.6 0.0 copy-done.3
  15.6 0.5 fusion.51
  16.2 1.3 fusion.79
  17.5 2.1 convolution_add_fusion.5
  19.5 3.3 %fusion.54 = (bf16[544,512]{1,0:T(8,128)(2,1)}, bf16[544,512]{1,0:T(8,128)(2,1)}) fusion(bf16[3,256,512]{2,1,0:T(8,128)(2,1)} %param.10, f32[544,256]{1,0:T(8,128)} %convolution_add_fusion.5, bf16[546,512]{1,0:T(8,128)(2,1)S(1)} %fusion.51, bf16[3,3,512,256]{3,2,1,0:T(8,128)(2,1)} %param.9, bf16[512,512]{1,0:T(8,128)(2,1)S(1)} %copy-done.3, ...), kind=kOutput, calls=%fused_computation.68 | convolution fusion | flops 288972800 | bytes 3317760 | tf_op jit(solution)/shard_map/dot_general | solution.py:28
  22.8 1.4 fusion.74
  24.3 1.4 convolution_add_fusion.3
  25.7 3.3 %fusion.56 = (bf16[538,512]{1,0:T(8,128)(2,1)S(1)}, bf16[538,512]{1,0:T(8,128)(2,1)}) fusion(bf16[3,256,512]{2,1,0:T(8,128)(2,1)} %param.10, f32[538,256]{1,0:T(8,128)S(1)} %convolution_add_fusion.3, bf16[544,512]{1,0:T(8,128)(2,1)} %get-tuple-element.20, bf16[3,3,512,256]{3,2,1,0:T(8,128)(2,1)} %param.9, bf16[544,512]{1,0:T(8,128)(2,1)} %get-tuple-element.21), kind=kOutput, calls=%fused_computation.70 | convolution fusion | flops 284959232 | bytes 3291136 | tf_op jit(solution)/shard_map/dot_general | solution.py:28
  29.0 1.2 fusion.86
  30.3 1.3 convolution_add_fusion.7
  31.6 3.1 %fusion.58 = bf16[520,512]{1,0:T(8,128)(2,1)} fusion(f32[520,256]{1,0:T(8,128)S(1)} %convolution_add_fusion.7, bf16[538,512]{1,0:T(8,128)(2,1)S(1)} %get-tuple-element.22, bf16[538,512]{1,0:T(8,128)(2,1)} %get-tuple-element.23, bf16[3,256,512]{2,1,0:T(8,128)(2,1)} %param.10, bf16[3,3,512,256]{3,2,1,0:T(8,128)(2,1)} %param.9), kind=kOutput, calls=%fused_computation.73 | convolution fusion | flops 275425280 | bytes 2654208 | tf_op jit(solution)/shard_map/dot_general | solution.py:28
  34.7 2.1 fusion.147
  36.7 0.2 slice.166
  37.0 1.3 slice.163
  38.3 3.0 %fusion.156 = f32[64,512]{1,0:T(8,128)S(1)} fusion(bf16[64,4096]{1,0:T(8,128)(2,1)S(1)} %slice.163, bf16[4096,512]{1,0:T(8,128)(2,1)} %bitcast.129), kind=kOutput, calls=%fused_computation.160 | convolution fusion | flops 268435456 | bytes 4849664 | tf_op jit(solution)/shard_map/dot_general | solution.py:47
  41.3 5.9 %convolution_convert_fusion.1 = bf16[64,4096]{1,0:T(8,128)(2,1)} fusion(bf16[512,4096]{1,0:T(8,128)(2,1)} %param.12, f32[64,512]{1,0:T(8,128)S(1)} %fusion.156, bf16[64,4096]{1,0:T(8,128)(2,1)S(1)} %slice.166, bf16[4096,512]{1,0:T(8,128)(2,1)} %bitcast.128), kind=kOutput, calls=%fused_computation.6 | convolution fusion | flops 537198592 | bytes 9568256 | tf_op jit(solution)/shard_map/dot_general | solution.py:50
  47.2 0.0 copy-start.6
  47.2 0.0 all-gather.4.cloned.1.call-update
  47.2 0.0 all-gather.8.cloned.1.call-start
  47.3 48.4 %all-gather.4.cloned.1.call-done = bf16[512,4096]{1,0:T(8,128)(2,1)} async-done(((bf16[64,4096]{1,0:T(8,128)(2,1)}), bf16[512,4096]{1,0:T(8,128)(2,1)}) %all-gather.4.cloned.1.call-update) | async-done | bytes 4194320 | tf_op jit(solution)/shard_map/all_gather | solution.py:51
  95.7 0.0 copy-start.2
  95.7 3.2 %fusion = f32[512]{0:T(512)S(1)} fusion(bf16[512,4096]{1,0:T(8,128)(2,1)} %all-gather.4.cloned.1.call-done), kind=kLoop, calls=%fused_computation.2 | loop fusion | flops 6290944 | bytes 4196352 | tf_op jit(solution)/shard_map/reduce_sum | solution.py:53
  98.9 0.0 copy-done.6
  98.9 0.2 copy-done.2
  99.1 3.6 %fusion.47 = bf16[512,256]{1,0:T(8,128)(2,1)} fusion(bf16[3,4096,256]{2,1,0:T(8,128)(2,1)} %param.14, bf16[512,4096]{1,0:T(8,128)(2,1)S(1)} %copy-done.2, f32[4096]{0:T(1024)S(1)} %copy-done.6, f32[512]{0:T(512)S(1)} %add_rsqrt_fusion), kind=kOutput, calls=%fused_computation.62 | convolution fusion | flops 1082261504 | bytes 6572032 | tf_op jit(solution)/shard_map/dot_general | solution.py:56
  102.7 0.0 all-gather.8.cloned.1.call-update
  102.8 0.0 all-gather.6.cloned.1.call-start
  102.8 4.9 %fusion.44 = bf16[512,256]{1,0:T(8,128)(2,1)} fusion(bf16[3,4096,256]{2,1,0:T(8,128)(2,1)} %param.14, bf16[512,4096]{1,0:T(8,128)(2,1)} %all-gather.4.cloned.1.call-done, f32[4096]{0:T(1024)S(1)} %copy-done.6, f32[512]{0:T(512)S(1)} %add_rsqrt_fusion), kind=kOutput, calls=%fused_computation.61 | convolution fusion | flops 1082261504 | bytes 6572032 | tf_op jit(solution)/shard_map/dot_general | solution.py:56
  107.7 0.0 all-gather.6.cloned.1.call-update
  107.7 0.2 reduce-scatter.2.cloned.1.call-start
  108.0 0.7 broadcast_compare_fusion
  108.6 4.6 %fusion.41 = bf16[512,256]{0,1:T(8,128)(2,1)S(1)} fusion(bf16[3,4096,256]{2,1,0:T(8,128)(2,1)} %param.14, bf16[512,4096]{1,0:T(8,128)(2,1)} %all-gather.4.cloned.1.call-done, f32[4096]{0:T(1024)S(1)} %copy-done.6, f32[512]{0:T(512)S(1)} %add_rsqrt_fusion), kind=kOutput, calls=%fused_computation.60 | convolution fusion | flops 1082261504 | bytes 6572032 | tf_op jit(solution)/shard_map/dot_general | solution.py:56
  113.2 14.1 %all-gather.8.cloned.1.call-done = bf16[2048,256]{1,0:T(8,128)(2,1)} async-done(((bf16[512,256]{1,0:T(8,128)(2,1)}), bf16[2048,256]{1,0:T(8,128)(2,1)}) %all-gather.8.cloned.1.call-update) | async-done | bytes 1048592 | tf_op jit(solution)/shard_map/all_gather | solution.py:76
  127.3 2.3 fusion.146
  129.6 2.0 copy.18
  131.6 2.1 copy.17
  133.7 22.1 %all-gather.6.cloned.1.call-done = bf16[2048,256]{1,0:T(8,128)(2,1)} async-done(((bf16[512,256]{1,0:T(8,128)(2,1)}), bf16[2048,256]{1,0:T(8,128)(2,1)}) %all-gather.6.cloned.1.call-update) | async-done | bytes 1048592 | tf_op jit(solution)/shard_map/all_gather | solution.py:75
  155.8 1.4 slice_bitcast_fusion
  157.2 1.2 fusion.4
  158.4 1.2 fusion.3
  159.6 0.0 copy-start.5
  159.6 3.0 %fusion.5 = (f32[2,512]{1,0:T(2,128)S(1)}, f32[2,512]{1,0:T(2,128)S(1)}) fusion(f32[2,512,1024]{2,1,0:T(8,128)S(1)} %get-tuple-element.27, f32[2,512]{1,0:T(2,128)S(1)} %get-tuple-element.17, pred[512,1024]{1,0:T(8,128)(4,1)S(1)} %get-tuple-element.19, f32[2,512]{1,0:T(2,128)S(1)} %get-tuple-element.16, f32[2,512,1024]{2,1,0:T(8,128)S(1)} %get-tuple-element.25, ...), kind=kLoop, calls=%fused_computation.21 | loop fusion | flops 10483712 | bytes 9453568 | tf_op jit(solution)/shard_map/reduce_sum | solution.py:95
  162.6 0.0 copy-done.5
  162.6 0.0 copy-start.4
  162.6 1.4 fusion.38
  164.1 0.0 copy-done.4
  164.1 1.6 fusion.62
  165.6 0.0 copy-done
  165.6 0.0 copy-start.1
  165.7 3.2 %convolution_convert_fusion = bf16[512,4096]{1,0:T(8,128)(2,1)} fusion(bf16[512,256]{0,1:T(8,128)(2,1)S(1)} %bitcast.132, bf16[256,4096]{1,0:T(8,128)(2,1)S(1)} %copy-done), kind=kOutput, calls=%fused_computation.5 | convolution fusion | flops 1075838976 | bytes 6553600 | tf_op jit(solution)/shard_map/dot_general | solution.py:108
  168.9 0.0 reduce-scatter.2.cloned.1.call-update
  168.9 51.1 %reduce-scatter.2.cloned.1.call-done = bf16[64,4096]{1,0:T(8,128)(2,1)} async-done(((bf16[512,4096]{1,0:T(8,128)(2,1)}), bf16[64,4096]{1,0:T(8,128)(2,1)}) %reduce-scatter.2.cloned.1.call-update) | async-done | bytes 524304 | tf_op jit(solution)/shard_map/reduce_scatter | solution.py:107
  220.0 0.0 copy-done.1
  220.0 2.0 add_convert_fusion.1
  (5 shorter events, 0.0 us)
Async XLA Ops:
  6.5 159.1 %copy-start = (bf16[256,4096]{1,0:T(8,128)(2,1)S(1)}, bf16[256,4096]{1,0:T(8,128)(2,1)}, u32[]{:S(2)}) copy-start(bf16[256,4096]{1,0:T(8,128)(2,1)} %param.15) | copy-start | bytes 6291460
  6.5 89.1 %all-gather.4.cloned.1.call-start = ((), (), s32[]{:S(2)}) async-start(), calls=%async_computation.1 | async-start | bytes 4718592 | tf_op jit(solution)/shard_map/all_gather | solution.py:51
  7.5 8.2 %copy-start.3 = (bf16[512,512]{1,0:T(8,128)(2,1)S(1)}, bf16[512,512]{1,0:T(8,128)(2,1)}, u32[]{:S(2)}) copy-start(bf16[512,512]{1,0:T(8,128)(2,1)} %param.8) | copy-start | bytes 1572868
  7.5 8.1 %collective-permute-start = (bf16[34,512]{1,0:T(8,128)(2,1)S(1)}, bf16[34,512]{1,0:T(8,128)(2,1)S(1)}, u32[]{:S(2)}, u32[]{:S(2)}) collective-permute-start(bf16[34,512]{1,0:T(8,128)(2,1)S(1)} %slice.137), channel_id=1, source_target_pairs={{0,1},{1,2},{2,3},{3,4},{4,5},{5,6},{6,7},{7,8},{8,9},{9,10},{10,1... | collective-permute-start | bytes 104456 | tf_op jit(solution)/shard_map/ppermute | solution.py:13
  47.2 51.7 %copy-start.6 = (f32[4096]{0:T(1024)S(1)}, f32[4096]{0:T(1024)}, u32[]{:S(2)}) copy-start(f32[4096]{0:T(1024)} %param.13) | copy-start | bytes 49156
  47.2 80.1 %all-gather.8.cloned.1.call-start = ((), (), s32[]{:S(2)}) async-start(), calls=%async_computation.3 | async-start | bytes 1310720 | tf_op jit(solution)/shard_map/all_gather | solution.py:76
  95.7 3.4 %copy-start.2 = (bf16[512,4096]{1,0:T(8,128)(2,1)S(1)}, bf16[512,4096]{1,0:T(8,128)(2,1)}, u32[]{:S(2)}) copy-start(bf16[512,4096]{1,0:T(8,128)(2,1)} %all-gather.4.cloned.1.call-done) | copy-start | bytes 12582916
  102.8 53.1 %all-gather.6.cloned.1.call-start = ((), (), s32[]{:S(2)}) async-start(), calls=%async_computation.2 | async-start | bytes 1310720 | tf_op jit(solution)/shard_map/all_gather | solution.py:75
  107.7 112.3 %reduce-scatter.2.cloned.1.call-start = ((), (), s32[]{:S(2)}) async-start(), calls=%async_computation.4 | async-start | bytes 4718592 | tf_op jit(solution)/shard_map/reduce_scatter | solution.py:107
  159.6 3.0 %copy-start.5 = (bf16[1024,256]{0,1:T(8,128)(2,1)S(1)}, bf16[1024,256]{0,1:T(8,128)(2,1)}, u32[]{:S(2)}) copy-start(bf16[1024,256]{0,1:T(8,128)(2,1)} %copy.17) | copy-start | bytes 1572868
  162.6 1.4 copy-start.4
  165.6 54.3 %copy-start.1 = (bf16[64,4096]{1,0:T(8,128)(2,1)S(1)}, bf16[64,4096]{1,0:T(8,128)(2,1)}, u32[]{:S(2)}) copy-start(bf16[64,4096]{1,0:T(8,128)(2,1)} %convolution_convert_fusion.1) | copy-start | bytes 1572868
Sparse Core Ops, SparseCore 0:
  47.3 48.2 all-gather.3
  102.9 24.4 all-gather.7
  129.2 26.6 all-gather.5
  169.0 50.8 reduce-scatter.1
where the time goes:
time: 231 us; the launch traced here: 228 us
  waiting for transfers between devices  136 us (59%)
  matrix products  49 us (21%)
  local copies, waits for them, and re-layouts  18.2 us (8%)
  between operations  13.3 us (6%)
  other arithmetic  9.4 us (4%)
  starting transfers between devices  2.36 us (1%)
    reduce_scatter x1, waiting for transfers between devices, body(): lax.psum_scatter(jnp.dot(attn, out_weight, preferred_element_type=jnp.flo...  51.1 us
    all_gather x1, waiting for transfers between devices, body(): lax.all_gather(frames_mine, 'mp', axis=0, tiled=True).astype(jnp.float32)  48.4 us
    all_gather x1, waiting for transfers between devices, body(): key_piece = lax.all_gather(keys, 'seq', axis=0, tiled=True)  22.1 us
    all_gather x1, waiting for transfers between devices, body(): value_piece = lax.all_gather(values, 'seq', axis=0, tiled=True)  14.1 us
    dot_general x3, matrix products, body(): jnp.dot(normed, qkv_weight[index], preferred_element_type=jnp.float32)  13.1 us
    dot_general x3, matrix products, unit_apply(): jnp.dot(inner, second, preferred_element_type=jnp.float32)  9.74 us
    dot_general x1, matrix products, body(): jnp.dot(latent, in_proj, preferred_element_type=jnp.float32)  5.91 us
    slice x1, local copies, waits for them, and re-layouts, body(): taps[1]  5.74 us
  transfers between devices with their start and end apart: 5, of which 5 were waited for; matrix products, arithmetic and copies ran while one was open for 10% of the time, Pallas kernels for 0%

commit v1 on v0

--- a/solution.py
+++ b/solution.py
@@ -48,16 +48,21 @@
         + jnp.dot(grouped[1:], taps[1], preferred_element_type=jnp.float32)
     ).astype(jnp.bfloat16)
     frames_mine = jnp.dot(latent, in_proj, preferred_element_type=jnp.float32).astype(jnp.bfloat16)
-    wide = lax.all_gather(frames_mine, "mp", axis=0, tiled=True).astype(jnp.float32)
-    normed = (
-        wide * lax.rsqrt(jnp.mean(wide * wide, axis=1, keepdims=True) + 1e-05) * norm_gain
-    ).astype(jnp.bfloat16)
-    outputs = [
-        jnp.dot(normed, qkv_weight[index], preferred_element_type=jnp.float32).astype(jnp.bfloat16)
+    wide = frames_mine.astype(jnp.float32)
+    inverse = lax.rsqrt(jnp.mean(wide * wide, axis=1, keepdims=True) + 1e-05)
+    scaled = (latent.astype(jnp.float32) * inverse).astype(jnp.bfloat16)
+    everyone = lax.all_gather(scaled, ("seq", "mp"), axis=0, tiled=True)
+    gained = (in_proj.astype(jnp.float32) * norm_gain).astype(jnp.bfloat16)
+    folded = [
+        jnp.dot(gained, qkv_weight[index], preferred_element_type=jnp.float32).astype(jnp.bfloat16)
         for index in range(3)
     ]
-    stacked = jnp.stack(outputs, axis=0)
-    query, keys, values = (stacked[0], stacked[1], stacked[2])
+    shard = everyone.shape[0] // lax.axis_size("seq")
+    mine = lax.dynamic_slice_in_dim(everyone, lax.axis_index("seq") * shard, shard, 0)
+    query, key_piece, value_piece = (
+        jnp.dot(rows_of, weight, preferred_element_type=jnp.float32).astype(jnp.bfloat16)
+        for rows_of, weight in zip((mine, everyone, everyone), folded)
+    )
     length = query.shape[0]
     columns = query.shape[1]
     local_heads = columns // HD
@@ -72,8 +77,6 @@
     )
     carry = init
     start = jnp.int32(0)
-    key_piece = lax.all_gather(keys, "seq", axis=0, tiled=True)
-    value_piece = lax.all_gather(values, "seq", axis=0, tiled=True)
     rows = key_piece.shape[0]
     nblock = max(1, rows // 1024)
     blen = rows // nblock

time: 231 us -> 201 us (0.87)
  waiting for transfers between devices: 136 us -> 106 us
  matrix products: 49 us -> 53.6 us
  local copies, waits for them, and re-layouts: 18.2 us -> 15.5 us
  other arithmetic: 9.4 us -> 7.08 us
    all_gather x3 -> x1, waiting for transfers between devices: 84.7 us -> 56 us  [body(): everyone = lax.all_gather(scaled, ('seq', 'mp'), axis=0, tiled=True)]
    dot_general x3 -> x4, matrix products: 13.1 us -> 20.4 us  [the longest x3 19.6 us: body(): jnp.dot(rows_of, weight, preferred_element_type=jnp.float32)]
    reshape x2 -> x0, local copies, waits for them, and re-layouts: 4.12 us -> none  [body(): value_piece[index * blen:(index + 1) * blen].reshape(blen, local_heads, HD)]
    dot_general x1, matrix products: 5.91 us -> 1.91 us  [body(): jnp.dot(latent, in_proj, preferred_element_type=jnp.float32)]
    reduce_sum x1 -> x0, other arithmetic: 3.23 us -> none  [body(): jnp.mean(wide * wide, axis=1, keepdims=True) + 1e-05]
  transfers between devices with their start and end apart: 5 -> 3, of which waited for: 5 -> 3; matrix products, arithmetic and copies ran while one was open for 10% -> 3% of each run, Pallas kernels for 0% -> 0%
where the time goes in v1:
time: 201 us; the launch traced here: 198 us
  waiting for transfers between devices  106 us (53%)
  matrix products  53.6 us (27%)
  local copies, waits for them, and re-layouts  15.5 us (8%)
  between operations  13.6 us (7%)
  other arithmetic  7.08 us (4%)
  starting transfers between devices  2.28 us (1%)
    all_gather x1, waiting for transfers between devices, body(): everyone = lax.all_gather(scaled, ('seq', 'mp'), axis=0, tiled=True)  56 us
    reduce_scatter x1, waiting for transfers between devices, body(): lax.psum_scatter(jnp.dot(attn, out_weight, preferred_element_type=jnp.flo...  49.9 us
    dot_general x3, matrix products, body(): jnp.dot(rows_of, weight, preferred_element_type=jnp.float32)  19.6 us
    dot_general x3, matrix products, unit_apply(): jnp.dot(inner, second, preferred_element_type=jnp.float32)  9.74 us
    slice x1, local copies, waits for them, and re-layouts, body(): taps[1]  5.74 us
    dot_general x3, matrix products, unit_apply(): jnp.dot(act[dilation:dilation + count], first[1], preferred_element_type=...  4.8 us
  transfers between devices with their start and end apart: 3, of which 3 were waited for; matrix products, arithmetic and copies ran while one was open for 3% of the time, Pallas kernels for 0%

profile of v1, /device:TPU:6, one launch (start us, length us, event | category | flops | bytes accessed | tf_op | source)
XLA Modules:
  0.0 198.4 jit_solution(18055996650600448555)
XLA Ops:
  6.5 0.0 copy-start
  6.5 0.0 all-gather.2.cloned.1.call-start
  6.5 0.9 slice.137
  7.5 0.0 copy-start.5
  7.5 2.1 %collective-permute-start = (bf16[34,512]{1,0:T(8,128)(2,1)S(1)}, bf16[34,512]{1,0:T(8,128)(2,1)S(1)}, u32[]{:S(2)}, u32[]{:S(2)}) collective-permute-start(bf16[34,512]{1,0:T(8,128)(2,1)S(1)} %slice.137), channel_id=1, source_target_pairs={{0,1},{1,2},{2,3},{3,4},{4,5},{5,6},{6,7},{7,8},{8,9},{9,10},{10,1... | collective-permute-start | bytes 104456 | tf_op jit(solution)/shard_map/ppermute | solution.py:13
  9.6 5.7 %fusion.142 = (bf16[8,512,512]{2,1,0:T(8,128)(2,1)}, bf16[8,512,512]{2,1,0:T(8,128)(2,1)}) fusion(bf16[16,512,512]{2,1,0:T(8,128)(2,1)} %param.11), kind=kLoop, calls=%fused_computation.153 | loop fusion | bytes 16777216 | tf_op jit(solution)/shard_map/slice | solution.py:48
  15.3 0.4 collective-permute-done
  15.6 0.0 copy-done.5
  15.6 0.5 fusion.49
  16.2 1.3 fusion.83
  17.5 2.1 %convolution_add_fusion.5 = f32[544,256]{1,0:T(8,128)} fusion(f32[544,256]{1,0:T(8,128)S(1)} %fusion.83, bf16[546,512]{1,0:T(8,128)(2,1)S(1)} %fusion.49, bf16[3,3,512,256]{3,2,1,0:T(8,128)(2,1)} %param.9), kind=kOutput, calls=%fused_computation.51 | convolution fusion | flops 142745600 | bytes 1933312 | tf_op jit(solution)/shard_map/dot_general | solution.py:20
  19.5 3.3 %fusion.54 = (bf16[544,512]{1,0:T(8,128)(2,1)}, bf16[544,512]{1,0:T(8,128)(2,1)}) fusion(bf16[3,256,512]{2,1,0:T(8,128)(2,1)} %param.10, f32[544,256]{1,0:T(8,128)} %convolution_add_fusion.5, bf16[546,512]{1,0:T(8,128)(2,1)S(1)} %fusion.49, bf16[3,3,512,256]{3,2,1,0:T(8,128)(2,1)} %param.9, bf16[512,512]{1,0:T(8,128)(2,1)S(1)} %copy-done.5, ...), kind=kOutput, calls=%fused_computation.68 | convolution fusion | flops 288972800 | bytes 3317760 | tf_op jit(solution)/shard_map/dot_general | solution.py:28
  22.9 1.4 fusion.78
  24.3 1.4 convolution_add_fusion.3
  25.7 3.3 %fusion.56 = (bf16[538,512]{1,0:T(8,128)(2,1)S(1)}, bf16[538,512]{1,0:T(8,128)(2,1)}) fusion(bf16[3,256,512]{2,1,0:T(8,128)(2,1)} %param.10, f32[538,256]{1,0:T(8,128)S(1)} %convolution_add_fusion.3, bf16[544,512]{1,0:T(8,128)(2,1)} %get-tuple-element.20, bf16[3,3,512,256]{3,2,1,0:T(8,128)(2,1)} %param.9, bf16[544,512]{1,0:T(8,128)(2,1)} %get-tuple-element.21), kind=kOutput, calls=%fused_computation.70 | convolution fusion | flops 284959232 | bytes 3291136 | tf_op jit(solution)/shard_map/dot_general | solution.py:28
  29.1 1.2 fusion.90
  30.3 1.3 convolution_add_fusion.7
  31.6 3.1 %fusion.58 = bf16[520,512]{1,0:T(8,128)(2,1)} fusion(f32[520,256]{1,0:T(8,128)S(1)} %convolution_add_fusion.7, bf16[538,512]{1,0:T(8,128)(2,1)S(1)} %get-tuple-element.22, bf16[538,512]{1,0:T(8,128)(2,1)} %get-tuple-element.23, bf16[3,256,512]{2,1,0:T(8,128)(2,1)} %param.10, bf16[3,3,512,256]{3,2,1,0:T(8,128)(2,1)} %param.9), kind=kOutput, calls=%fused_computation.73 | convolution fusion | flops 275425280 | bytes 2654208 | tf_op jit(solution)/shard_map/dot_general | solution.py:28
  34.7 2.1 %fusion.145 = (bf16[512,512]{1,0:T(8,128)(2,1)S(1)}, bf16[512,512]{1,0:T(8,128)(2,1)}) fusion(bf16[520,512]{1,0:T(8,128)(2,1)} %fusion.58), kind=kLoop, calls=%fused_computation.156 | loop fusion | bytes 2097152 | tf_op jit(solution)/shard_map/slice | solution.py:48
  36.8 0.2 slice.166
  37.0 1.3 slice.163
  38.3 0.0 copy-start.1
  38.3 0.0 copy-start.2
  38.3 3.2 %fusion.154 = f32[64,512]{1,0:T(8,128)S(1)} fusion(bf16[64,4096]{1,0:T(8,128)(2,1)S(1)} %slice.163, bf16[4096,512]{1,0:T(8,128)(2,1)} %bitcast.128), kind=kOutput, calls=%fused_computation.157 | convolution fusion | flops 268435456 | bytes 4849664 | tf_op jit(solution)/shard_map/dot_general | solution.py:47
  41.5 0.3 copy-done.1
  41.7 0.8 fusion.50
  42.6 0.4 copy-done.2
  43.0 0.0 copy-start.8
  43.0 1.9 multiply_reduce_fusion
  45.0 0.7 multiply_convert_fusion.16
  45.7 0.0 all-gather.2.cloned.1.call-update
  45.7 0.2 reduce-scatter.2.cloned.1.call-start
  46.0 0.7 broadcast_compare_fusion
  46.6 56.0 %all-gather.2.cloned.1.call-done = bf16[2048,512]{1,0:T(8,128)(2,1)} async-done(((bf16[64,512]{1,0:T(8,128)(2,1)}), bf16[2048,512]{1,0:T(8,128)(2,1)}) %all-gather.2.cloned.1.call-update) | async-done | bytes 2097168 | tf_op jit(solution)/shard_map/all_gather | solution.py:54
  102.6 0.0 copy-done.8
  102.6 7.4 %convolution_convert_fusion.3 = bf16[2048,256]{0,1:T(8,128)(2,1)} fusion(bf16[2048,512]{1,0:T(8,128)(2,1)} %all-gather.2.cloned.1.call-done, bf16[3,4096,256]{2,1,0:T(8,128)(2,1)} %param.14, bf16[512,4096]{1,0:T(8,128)(2,1)} %param.12, f32[4096]{0:T(1024)S(1)} %copy-done.8), kind=kOutput, calls=%fused_computation.26 | convolution fusion | flops 1617559552 | bytes 9453568 | tf_op jit(solution)/shard_map/dot_general | solution.py:63
  110.0 2.3 %fusion.144 = (bf16[1024,256]{0,1:T(8,128)(2,1)}, bf16[1024,256]{0,1:T(8,128)(2,1)}) fusion(bf16[2048,256]{0,1:T(8,128)(2,1)} %convolution_convert_fusion.3), kind=kLoop, calls=%fused_computation.155 | loop fusion | bytes 2097152 | tf_op jit(solution)/shard_map/slice | solution.py:85
  112.3 7.4 %convolution_convert_fusion.2 = bf16[2048,256]{0,1:T(8,128)(2,1)} fusion(bf16[2048,512]{1,0:T(8,128)(2,1)} %all-gather.2.cloned.1.call-done, bf16[3,4096,256]{2,1,0:T(8,128)(2,1)} %param.14, bf16[512,4096]{1,0:T(8,128)(2,1)} %param.12, f32[4096]{0:T(1024)S(1)} %copy-done.8), kind=kOutput, calls=%fused_computation.25 | convolution fusion | flops 1617559552 | bytes 9453568 | tf_op jit(solution)/shard_map/dot_general | solution.py:63
  119.7 2.3 %fusion.143 = (bf16[1024,256]{0,1:T(8,128)(2,1)}, bf16[1024,256]{0,1:T(8,128)(2,1)}) fusion(bf16[2048,256]{0,1:T(8,128)(2,1)} %convolution_convert_fusion.2), kind=kLoop, calls=%fused_computation.154 | loop fusion | bytes 2097152 | tf_op jit(solution)/shard_map/slice | solution.py:86
  121.9 4.8 %convolution_convert_fusion.4 = bf16[512,256]{0,1:T(8,128)(2,1)S(1)} fusion(bf16[3,4096,256]{2,1,0:T(8,128)(2,1)} %param.14, bf16[512,4096]{1,0:T(8,128)(2,1)} %param.12, f32[4096]{0:T(1024)S(1)} %copy-done.8, bf16[2048,512]{1,0:T(8,128)(2,1)} %all-gather.2.cloned.1.call-done, s32[]{:T(128)S(6)} %select_n.100), kind=kOutput, calls=%fused_computation.62 | convolution fusion | flops 1214513152 | bytes 7094276 | tf_op jit(solution)/shard_map/dot_general | solution.py:63
  126.7 0.0 copy-start.4
  126.7 2.3 %fusion.1 = (f32[2,512]{1,0:T(2,128)S(1)}, f32[2,512,1024]{2,1,0:T(8,128)S(1)}) fusion(pred[512,1024]{1,0:T(8,128)(4,1)S(1)} %get-tuple-element.19, bf16[512,2,128]{0,2,1:T(8,128)(2,1)S(1)} %bitcast.131, bf16[1024,2,128]{0,2,1:T(8,128)(2,1)} %bitcast.130), kind=kOutput, calls=%fused_computation.8 | convolution fusion | flops 271580160 | bytes 5509120 | tf_op jit(solution)/shard_map/qhd,khd->hqk/dot_general | solution.py:89
  129.0 0.0 copy-done.4
  129.0 1.2 fusion.2
  130.2 0.0 copy-start.7
  130.2 3.2 %fusion.6 = (f32[2,512]{1,0:T(2,128)S(1)}, f32[2,512]{1,0:T(2,128)S(1)}) fusion(f32[2,512,1024]{2,1,0:T(8,128)S(1)} %get-tuple-element.29, f32[2,512]{1,0:T(2,128)S(1)} %get-tuple-element.17, pred[512,1024]{1,0:T(8,128)(4,1)S(1)} %get-tuple-element.19, f32[2,512]{1,0:T(2,128)S(1)} %get-tuple-element.16, f32[2,512,1024]{2,1,0:T(8,128)S(1)} %get-tuple-element.27, ...), kind=kLoop, calls=%fused_computation.21 | loop fusion | flops 10483712 | bytes 9453568 | tf_op jit(solution)/shard_map/reduce_sum | solution.py:98
  133.4 0.0 copy-done.7
  133.5 0.0 copy-start.6
  133.5 1.4 fusion.36
  134.9 0.0 copy-done.6
  134.9 1.6 fusion.66
  136.4 0.0 copy-done
  136.5 0.0 copy-start.3
  136.5 3.2 %convolution_convert_fusion = bf16[512,4096]{1,0:T(8,128)(2,1)} fusion(bf16[512,256]{0,1:T(8,128)(2,1)S(1)} %bitcast.135, bf16[256,4096]{1,0:T(8,128)(2,1)S(1)} %copy-done), kind=kOutput, calls=%fused_computation.1 | convolution fusion | flops 1075838976 | bytes 6553600 | tf_op jit(solution)/shard_map/dot_general | solution.py:111
  139.7 0.0 reduce-scatter.2.cloned.1.call-update
  139.7 49.9 %reduce-scatter.2.cloned.1.call-done = bf16[64,4096]{1,0:T(8,128)(2,1)} async-done(((bf16[512,4096]{1,0:T(8,128)(2,1)}), bf16[64,4096]{1,0:T(8,128)(2,1)}) %reduce-scatter.2.cloned.1.call-update) | async-done | bytes 524304 | tf_op jit(solution)/shard_map/reduce_scatter | solution.py:110
  189.6 0.0 copy-done.3
  189.6 1.9 add_convert_fusion.1
  (5 shorter events, 0.0 us)
Async XLA Ops:
  6.5 129.9 %copy-start = (bf16[256,4096]{1,0:T(8,128)(2,1)S(1)}, bf16[256,4096]{1,0:T(8,128)(2,1)}, u32[]{:S(2)}) copy-start(bf16[256,4096]{1,0:T(8,128)(2,1)} %param.15) | copy-start | bytes 6291460
  6.5 96.1 %all-gather.2.cloned.1.call-start = ((), (), s32[]{:S(2)}) async-start(), calls=%async_computation.1 | async-start | bytes 2162688 | tf_op jit(solution)/shard_map/all_gather | solution.py:54
  7.5 8.2 %copy-start.5 = (bf16[512,512]{1,0:T(8,128)(2,1)S(1)}, bf16[512,512]{1,0:T(8,128)(2,1)}, u32[]{:S(2)}) copy-start(bf16[512,512]{1,0:T(8,128)(2,1)} %param.8) | copy-start | bytes 1572868
  7.5 8.1 %collective-permute-start = (bf16[34,512]{1,0:T(8,128)(2,1)S(1)}, bf16[34,512]{1,0:T(8,128)(2,1)S(1)}, u32[]{:S(2)}, u32[]{:S(2)}) collective-permute-start(bf16[34,512]{1,0:T(8,128)(2,1)S(1)} %slice.137), channel_id=1, source_target_pairs={{0,1},{1,2},{2,3},{3,4},{4,5},{5,6},{6,7},{7,8},{8,9},{9,10},{10,1... | collective-permute-start | bytes 104456 | tf_op jit(solution)/shard_map/ppermute | solution.py:13
  38.3 3.5 %copy-start.1 = (bf16[8,512,512]{2,1,0:T(8,128)(2,1)S(1)}, bf16[8,512,512]{2,1,0:T(8,128)(2,1)}, u32[]{:S(2)}) copy-start(bf16[8,512,512]{2,1,0:T(8,128)(2,1)} %get-tuple-element.7) | copy-start | bytes 12582916
  38.3 4.7 %copy-start.2 = (bf16[512,4096]{1,0:T(8,128)(2,1)S(1)}, bf16[512,4096]{1,0:T(8,128)(2,1)}, u32[]{:S(2)}) copy-start(bf16[512,4096]{1,0:T(8,128)(2,1)} %param.12) | copy-start | bytes 12582916
  43.0 59.6 %copy-start.8 = (f32[4096]{0:T(1024)S(1)}, f32[4096]{0:T(1024)}, u32[]{:S(2)}) copy-start(f32[4096]{0:T(1024)} %param.13) | copy-start | bytes 49156
  45.7 143.9 %reduce-scatter.2.cloned.1.call-start = ((), (), s32[]{:S(2)}) async-start(), calls=%async_computation.2 | async-start | bytes 4718592 | tf_op jit(solution)/shard_map/reduce_scatter | solution.py:110
  126.7 2.3 %copy-start.4 = (bf16[1024,256]{0,1:T(8,128)(2,1)S(1)}, bf16[1024,256]{0,1:T(8,128)(2,1)}, u32[]{:S(2)}) copy-start(bf16[1024,256]{0,1:T(8,128)(2,1)} %get-tuple-element.11) | copy-start | bytes 1572868
  130.2 3.2 %copy-start.7 = (bf16[1024,256]{0,1:T(8,128)(2,1)S(1)}, bf16[1024,256]{0,1:T(8,128)(2,1)}, u32[]{:S(2)}) copy-start(bf16[1024,256]{0,1:T(8,128)(2,1)} %get-tuple-element.10) | copy-start | bytes 1572868
  133.5 1.4 copy-start.6
  136.5 53.2 %copy-start.3 = (f32[64,4096]{1,0:T(8,128)S(1)}, f32[64,4096]{1,0:T(8,128)}, u32[]{:S(2)}) copy-start(f32[64,4096]{1,0:T(8,128)} %get-tuple-element.25) | copy-start | bytes 3145732
Sparse Core Ops, SparseCore 0:
  45.8 56.7 all-gather.1
  139.9 49.7 reduce-scatter.1

commit v2 on v0

v2 whole, which is shorter than its diff:
```python
import functools

import jax
import jax.numpy as jnp
from jax import lax
from jax.experimental import pallas as pl
from jax.experimental.pallas import tpu as pltpu
from jax.sharding import PartitionSpec as P

HD = 128
STRIDE = 8
DILATIONS = (1, 3, 9)
HALO = -(-(2 * sum(DILATIONS) + STRIDE) // 16) * 16
MESH = pl.DeviceIdType.MESH
F32 = jnp.float32
BF16 = jnp.bfloat16


def dot(a, b):
    return jnp.dot(a, b, preferred_element_type=F32)


def elu(x):
    low = jnp.minimum(x, 0.0)
    near = low * (1.0 + low * (0.5 + low * (1.0 / 6.0)))
    return jnp.where(x > 0.0, x, jnp.where(low > -0.03, near, jnp.exp(low) - 1.0))


def front_kernel(
    n_seq,
    n_mp,
    audio,
    first_hbm,
    second_hbm,
    down_hbm,
    proj_hbm,
    gain,
    qkv_hbm,
    frames_out,
    attn_out,
    halo,
    first,
    second,
    down,
    proj,
    qkv,
    act,
    gath,
    folded,
    peak,
    total,
    accum,
    load_sem,
    halo_sem,
    send_sem,
    recv_sem,
):
    seq = lax.axis_index("seq")
    mp = lax.axis_index("mp")
    n_z = n_mp // 2
    z = mp // 2
    core = mp % 2
    twin = mp + 1 - 2 * core
    linear = seq * n_mp + mp
    count = n_seq * n_mp
    after = (linear + 1) % count
    before = (linear + count - 1) % count
    rows = audio.shape[0]
    frames = gath.shape[1]
    channels = gath.shape[2]
    columns = folded.shape[2]
    heads = columns // HD

    loads = [
        pltpu.make_async_copy(src, dst, load_sem.at[i])
        for i, (src, dst) in enumerate(
            (
                (first_hbm, first),
                (second_hbm, second),
                (down_hbm, down),
                (proj_hbm, proj),
                (qkv_hbm, qkv),
            )
        )
    ]
    for load in loads:
        load.start()

    def z_peer(j):
        return (seq, ((z + j) % n_z) * 2 + core)

    def seq_peer(j):
        return ((seq + j) % n_seq, mp)

    barrier = pltpu.get_barrier_semaphore()
    peers = [z_peer(j) for j in range(1, n_z)] + [seq_peer(j) for j in range(1, n_seq)]
    peers += [(seq, twin), (after // n_mp, after % n_mp), (before // n_mp, before % n_mp)]
    for peer in peers:
        pl.semaphore_signal(barrier, inc=1, device_id=peer, device_id_type=MESH)
    pl.semaphore_wait(barrier, len(peers))

    edge = pltpu.make_async_remote_copy(
        src_ref=audio.at[pl.ds(rows - HALO, HALO)],
        dst_ref=halo,
        send_sem=halo_sem.at[0],
        recv_sem=halo_sem.at[1],
        device_id=(after // n_mp, after % n_mp),
        device_id_type=MESH,
    )
    edge.start()
    edge.wait_recv()
    behind = jnp.where(linear == 0, 0.0, halo[...].astype(F32))
    state = jnp.concatenate([behind, audio[...].astype(F32)], axis=0)
    for unit, dilation in enumerate(DILATIONS):
        u = elu(state).astype(BF16)
        if unit == 0:
            loads[0].wait()
        middle = dot(u, first[unit, 2])
        middle = middle + pltpu.roll(dot(u, first[unit, 1]), dilation, 0)
        middle = middle + pltpu.roll(dot(u, first[unit, 0]), 2 * dilation, 0)
        v = elu(middle).astype(BF16)
        if unit == 0:
            loads[1].wait()
        state = (state + dot(v, second[unit])).astype(BF16).astype(F32)
    act[...] = elu(state)[HALO - STRIDE :].reshape(act.shape)
    loads[2].wait()
    latent = jnp.zeros((frames, channels), F32)
    for tap in range(2 * STRIDE):
        begin = tap // STRIDE
        piece = act[begin : begin + frames, tap % STRIDE, :].astype(BF16)
        latent = latent + dot(piece, down[tap])
    latent = latent.astype(BF16)
    loads[3].wait()
    wide = dot(latent, proj[...]).astype(BF16)
    frames_out[...] = wide
    wide = wide.astype(F32)
    inverse = lax.rsqrt(jnp.mean(wide * wide, axis=1, keepdims=True) + 1e-05)
    gath[linear] = (latent.astype(F32) * inverse).astype(BF16)

    def send(slot, row, column, device):
        return pltpu.make_async_remote_copy(
            src_ref=gath.at[slot],
            dst_ref=gath.at[slot],
            send_sem=send_sem.at[row, column],
            recv_sem=recv_sem.at[slot],
            device_id=device,
            device_id_type=MESH,
        )

    sent = []

    def begin_send(*args):
        copy = send(*args)
        copy.start()
        sent.append(copy)

    def arrived(slot):
        send(slot, 0, 0, (seq, twin)).wait_recv()

    for j in range(1, n_z):
        begin_send(linear, 0, n_seq + j, z_peer(j))
    for j in range(1, n_seq):
        begin_send(linear, 0, j, seq_peer(j))
    begin_send(linear, 0, 0, (seq, twin))

    loads[4].wait()
    folded[...] = jnp.zeros_like(folded)
    depth = qkv.shape[1]
    step = 512

    def fold(index, carry):
        at = pl.ds(pl.multiple_of(index * step, step), step)
        gained = (proj[:, at].astype(F32) * gain[:, at]).astype(BF16)
        for part in range(3):
            folded[part] += dot(gained, qkv[part, at, :])
        return carry

    lax.fori_loop(0, depth // step, fold, 0)

    for i in range(1, n_z):
        slot = seq * n_mp + ((z + n_z - i) % n_z) * 2 + core
        arrived(slot)
        for j in range(1, n_seq):
            begin_send(slot, i, j, seq_peer(j))
        begin_send(slot, i, 0, (seq, twin))
    for j in range(1, n_seq):
        for i in range(n_z):
            slot = ((seq + n_seq - j) % n_seq) * n_mp + ((z + n_z - i) % n_z) * 2 + core
            arrived(slot)
            begin_send(slot, j * n_z + i, 0, (seq, twin))
    for j in range(n_seq):
        for i in range(n_z):
            slot = ((seq + n_seq - j) % n_seq) * n_mp + ((z + n_z - i) % n_z) * 2 + 1 - core
            arrived(slot)

    length = n_mp * frames
    w_q = (folded[0] * HD ** (-0.5)).astype(BF16)
    w_k = folded[1].astype(BF16)
    w_v = folded[2].astype(BF16)

    def block(index):
        at = pl.ds(pl.multiple_of(index * n_mp, n_mp), n_mp)
        return gath[at].reshape(length, channels)

    query = dot(block(seq), w_q).astype(BF16)
    peak[...] = jnp.full_like(peak, -1e30)
    total[...] = jnp.zeros_like(total)
    accum[...] = jnp.zeros_like(accum)

    def attend(index, diagonal):
        source = block(index)
        keys = dot(source, w_k).astype(BF16)
        values = dot(source, w_v).astype(BF16)
        for head in range(heads):
            at = slice(head * HD, (head + 1) * HD)
            scores = lax.dot_general(
                query[:, at], keys[:, at], (((1,), (1,)), ((), ())), preferred_element_type=F32
            )
            if diagonal:
                q_pos = lax.broadcasted_iota(jnp.int32, scores.shape, 0)
                k_pos = lax.broadcasted_iota(jnp.int32, scores.shape, 1)
                scores = jnp.where(k_pos <= q_pos, scores, -1e30)
            old = peak[head]
            fresh = jnp.maximum(old, jnp.max(scores, axis=1, keepdims=True))
            probs = jnp.exp(scores - fresh)
            factor = jnp.exp(old - fresh)
            peak[head] = fresh
            total[head] = total[head] * factor + jnp.sum(probs, axis=1, keepdims=True)
            accum[head] = accum[head] * factor + dot(probs.astype(BF16), values[:, at])

    attend(seq, True)

    def earlier(index, carry):
        attend(index, False)
        return carry

    lax.fori_loop(0, seq, earlier, 0)
    for head in range(heads):
        attn_out[:, head * HD : (head + 1) * HD] = (accum[head] / total[head]).astype(BF16)

    edge.wait_send()
    for copy in sent:
        copy.wait_send()


def front(n_seq, n_mp, audio, first, second, down, proj, gain, qkv):
    rows, channels = audio.shape
    frames = rows // STRIDE
    width = proj.shape[1]
    columns = qkv.shape[2]
    heads = columns // HD
    length = frames * n_mp
    n_z = n_mp // 2
    vmem = pl.BlockSpec(memory_space=pltpu.VMEM)
    hbm = pl.BlockSpec(memory_space=pl.ANY)
    flops = 2 * channels * width * columns * 3 + 12 * rows * channels * channels
    return pl.pallas_call(
        functools.partial(front_kernel, n_seq, n_mp),
        out_shape=(
            jax.ShapeDtypeStruct((frames, width), BF16),
            jax.ShapeDtypeStruct((length, columns), BF16),
        ),
        in_specs=[vmem, hbm, hbm, hbm, hbm, vmem, hbm],
        out_specs=(vmem, vmem),
        scratch_shapes=[
            pltpu.VMEM((HALO, channels), BF16),
            pltpu.VMEM(first.shape, BF16),
            pltpu.VMEM(second.shape, BF16),
            pltpu.VMEM(down.shape, BF16),
            pltpu.VMEM(proj.shape, BF16),
            pltpu.VMEM(qkv.shape, BF16),
            pltpu.VMEM((frames + 1, STRIDE, channels), F32),
            pltpu.VMEM((n_seq * n_mp, frames, channels), BF16),
            pltpu.VMEM((3, channels, columns), F32),
            pltpu.VMEM((heads, length, 1), F32),
            pltpu.VMEM((heads, length, 1), F32),
            pltpu.VMEM((heads, length, HD), F32),
            pltpu.SemaphoreType.DMA((5,)),
            pltpu.SemaphoreType.DMA((2,)),
            pltpu.SemaphoreType.DMA((n_seq * n_z, n_seq + n_z)),
            pltpu.SemaphoreType.DMA((n_seq * n_mp,)),
        ],
        compiler_params=pltpu.CompilerParams(
            collective_id=0, has_side_effects=True, vmem_limit_bytes=56 * 2**20
        ),
        cost_estimate=pl.CostEstimate(flops=flops, bytes_accessed=24 * 2**20, transcendentals=0),
    )(audio, first, second, down, proj, gain, qkv)


def body(
    n_seq,
    n_mp,
    audio_feats,
    conv_first,
    conv_second,
    down_weight,
    in_proj,
    norm_gain,
    qkv_weight,
    out_weight,
):
    frames_mine, attn = front(
        n_seq,
        n_mp,
        audio_feats,
        conv_first,
        conv_second,
        down_weight,
        in_proj,
        norm_gain.reshape(1, -1),
        qkv_weight,
    )
    summed = lax.psum_scatter(
        dot(attn, out_weight).astype(BF16), "mp", scatter_dimension=0, tiled=True
    ).astype(F32)
    return (frames_mine.astype(F32) + summed).astype(BF16)


def solution(mesh):
    placed = (P(("seq", "mp"), None), P(), P(), P(), P(), P(), P(None, None, "mp"), P("mp", None))
    return jax.shard_map(
        functools.partial(body, mesh.shape["seq"], mesh.shape["mp"]),
        mesh=mesh,
        in_specs=placed,
        out_specs=P(("seq", "mp"), None),
        check_vma=False,
    )
```

time: 231 us -> 115 us (0.50)
  waiting for transfers between devices: 136 us -> 49.8 us
  matrix products: 49 us -> 4.21 us
  Pallas kernels: 0 us -> 43.6 us
  local copies, waits for them, and re-layouts: 18.2 us -> 0.01 us
  other arithmetic: 9.4 us -> 1.96 us
  starting transfers between devices: 2.36 us -> 0.01 us
    all_gather x3 -> x0, waiting for transfers between devices: 84.7 us -> none  [the longest x1 48.4 us: body(): lax.all_gather(frames_mine, 'mp', axis=0, tiled=True).astype(jnp.float32)]
    dot_general x19 -> x1, matrix products: 49 us -> 4.21 us  [dot(): return jnp.dot(a, b, preferred_element_type=F32)]
    pallas_call x0 -> x1, Pallas kernels: none -> 43.6 us  [front(): pl.pallas_call(functools.partial(front_kernel, n_seq, n_mp), out_shape=(j...]
    slice x6 -> x0, local copies, waits for them, and re-layouts: 12.5 us -> none  [the longest x1 5.74 us: body(): taps[1]]
    reduce_sum x2 -> x0, other arithmetic: 6.21 us -> none  [the longest x1 3.23 us: body(): jnp.mean(wide * wide, axis=1, keepdims=True) + 1e-05]
    reshape x2 -> x0, local copies, waits for them, and re-layouts: 4.12 us -> none  [body(): value_piece[index * blen:(index + 1) * blen].reshape(blen, local_heads, HD)]
  transfers between devices with their start and end apart: 5 -> 1, of which waited for: 5 -> 1; matrix products, arithmetic and copies ran while one was open for 10% -> 0% of each run, Pallas kernels for 0% -> 0%
where the time goes in v2:
time: 115 us; the launch traced here: 113 us
  waiting for transfers between devices  49.8 us (43%)
  Pallas kernels  43.6 us (38%)
  between operations  13.4 us (12%)
  matrix products  4.21 us (4%)
  other arithmetic  1.96 us (2%)
    reduce_scatter x1, waiting for transfers between devices, body(): lax.psum_scatter(dot(attn, out_weight).astype(BF16), 'mp', scatter_dimens...  49.7 us
    pallas_call x1, Pallas kernels, front(): pl.pallas_call(functools.partial(front_kernel, n_seq, n_mp), out_shape=(j...  43.6 us
    dot_general x1, matrix products, dot(): return jnp.dot(a, b, preferred_element_type=F32)  4.21 us
  transfers between devices with their start and end apart: 1, of which 1 were waited for; matrix products, arithmetic and copies ran while one was open for 0% of the time, Pallas kernels for 0%

profile of v2, /device:TPU:6, one launch (start us, length us, event | category | flops | bytes accessed | tf_op | source)
XLA Modules:
  0.0 112.9 jit_solution(12966265041834229427)
XLA Ops:
  6.5 0.0 copy-start
  6.5 0.0 reduce-scatter.2.cloned.1.call-start
  6.5 43.6 %shard_map.82 = (bf16[64,4096]{1,0:T(8,128)(2,1)}, bf16[512,256]{1,0:T(8,128)(2,1)}) custom-call(bf16[512,512]{1,0:T(8,128)(2,1)} %audio.1, bf16[3,3,512,256]{3,2,1,0:T(8,128)(2,1)} %first_hbm.1, bf16[3,256,512]{2,1,0:T(8,128)(2,1)} %second_hbm.1, bf16[16,512,512]{2,1,0:T(8,128)(2,1)} %down_hbm.1, bf16[512,4096]{1,0:T(8,128)(2,1)} %proj_hbm.1, ...), custom_call_target="tpu_custom_call" | custom-call | flops 4831838208 | bytes 25165824 | tf_op jit(solution)/shard_map/pallas_call | solution.py:257
  50.1 0.0 copy-done
  50.1 0.0 copy-start.1
  50.1 4.2 %convolution_convert_fusion = bf16[512,4096]{1,0:T(8,128)(2,1)} fusion(bf16[512,256]{1,0:T(8,128)(2,1)} %get-tuple-element.8, bf16[256,4096]{1,0:T(8,128)(2,1)S(1)} %copy-done), kind=kOutput, calls=%fused_computation | convolution fusion | flops 1075838976 | bytes 6553600 | tf_op jit(solution)/shard_map/dot_general | solution.py:20
  54.3 0.0 reduce-scatter.2.cloned.1.call-update
  54.4 49.7 %reduce-scatter.2.cloned.1.call-done = bf16[64,4096]{1,0:T(8,128)(2,1)} async-done(((bf16[512,4096]{1,0:T(8,128)(2,1)}), bf16[64,4096]{1,0:T(8,128)(2,1)}) %reduce-scatter.2.cloned.1.call-update) | async-done | bytes 524304 | tf_op jit(solution)/shard_map/reduce_scatter | solution.py:313
  104.1 0.0 copy-done.1
  104.1 2.0 %add_convert_fusion = bf16[64,4096]{1,0:T(8,128)(2,1)} fusion(bf16[64,4096]{1,0:T(8,128)(2,1)} %reduce-scatter.2.cloned.1.call-done, bf16[64,4096]{1,0:T(8,128)(2,1)S(1)} %copy-done.1), kind=kLoop, calls=%fused_computation.1 | loop fusion | flops 1048576 | bytes 1572864 | tf_op jit(solution)/shard_map/convert_element_type | solution.py:316
Async XLA Ops:
  6.5 43.6 %copy-start = (bf16[256,4096]{1,0:T(8,128)(2,1)S(1)}, bf16[256,4096]{1,0:T(8,128)(2,1)}, u32[]{:S(2)}) copy-start(bf16[256,4096]{1,0:T(8,128)(2,1)} %param.15) | copy-start | bytes 6291460
  6.5 97.6 %reduce-scatter.2.cloned.1.call-start = ((), (), s32[]{:S(2)}) async-start(), calls=%async_computation.1 | async-start | bytes 4718592 | tf_op jit(solution)/shard_map/reduce_scatter | solution.py:313
  50.1 54.0 %copy-start.1 = (bf16[64,4096]{1,0:T(8,128)(2,1)S(1)}, bf16[64,4096]{1,0:T(8,128)(2,1)}, u32[]{:S(2)}) copy-start(bf16[64,4096]{1,0:T(8,128)(2,1)} %get-tuple-element.7) | copy-start | bytes 1572868
Sparse Core Ops, SparseCore 0:
  54.5 49.5 reduce-scatter.1

commit v3 on v2

--- a/solution.py
+++ b/solution.py
@@ -11,6 +11,7 @@
 STRIDE = 8
 DILATIONS = (1, 3, 9)
 HALO = -(-(2 * sum(DILATIONS) + STRIDE) // 16) * 16
+CHUNKS = 4
 MESH = pl.DeviceIdType.MESH
 F32 = jnp.float32
 BF16 = jnp.bfloat16
@@ -26,7 +27,7 @@
     return jnp.where(x > 0.0, x, jnp.where(low > -0.03, near, jnp.exp(low) - 1.0))
 
 
-def front_kernel(
+def layer_kernel(
     n_seq,
     n_mp,
     audio,
@@ -36,8 +37,8 @@
     proj_hbm,
     gain,
     qkv_hbm,
-    frames_out,
-    attn_out,
+    out_hbm,
+    result,
     halo,
     first,
     second,
@@ -50,10 +51,24 @@
     peak,
     total,
     accum,
+    frames_mine,
+    frames_sum,
+    out_own,
+    out_twin,
+    out_pair,
+    attn_own,
+    attn_twin,
+    attn_pair,
+    leaving,
+    coming,
     load_sem,
     halo_sem,
     send_sem,
     recv_sem,
+    swap_send,
+    swap_recv,
+    chain_send,
+    chain_recv,
 ):
     seq = lax.axis_index("seq")
     mp = lax.axis_index("mp")
@@ -80,6 +95,7 @@
                 (down_hbm, down),
                 (proj_hbm, proj),
                 (qkv_hbm, qkv),
+                (out_hbm, out_own),
             )
         )
     ]
@@ -94,7 +110,10 @@
 
     barrier = pltpu.get_barrier_semaphore()
     peers = [z_peer(j) for j in range(1, n_z)] + [seq_peer(j) for j in range(1, n_seq)]
-    peers += [(seq, twin), (after // n_mp, after % n_mp), (before // n_mp, before % n_mp)]
+    pair = z + 1 - 2 * (z % 2)
+    pair_same = (seq, pair * 2 + core)
+    pair_other = (seq, pair * 2 + 1 - core)
+    peers += [(seq, twin), pair_other, (after // n_mp, after % n_mp), (before // n_mp, before % n_mp)]
     for peer in peers:
         pl.semaphore_signal(barrier, inc=1, device_id=peer, device_id_type=MESH)
     pl.semaphore_wait(barrier, len(peers))
@@ -108,6 +127,29 @@
         device_id_type=MESH,
     )
     edge.start()
+
+    def swap(index, src, dst, device):
+        return pltpu.make_async_remote_copy(
+            src_ref=src,
+            dst_ref=dst,
+            send_sem=swap_send.at[index],
+            recv_sem=swap_recv.at[index],
+            device_id=device,
+            device_id_type=MESH,
+        )
+
+    paired_width = out_pair.shape[2]
+    weight_swaps = [
+        swap(0, out_hbm, out_twin, (seq, twin)),
+        swap(
+            1,
+            out_hbm.at[:, pl.ds(out_hbm.shape[1] - paired_width, paired_width)],
+            out_pair.at[core],
+            pair_same,
+        ),
+    ]
+    for copy in weight_swaps:
+        copy.start()
     edge.wait_recv()
     behind = jnp.where(linear == 0, 0.0, halo[...].astype(F32))
     state = jnp.concatenate([behind, audio[...].astype(F32)], axis=0)
@@ -132,7 +174,7 @@
     latent = latent.astype(BF16)
     loads[3].wait()
     wide = dot(latent, proj[...]).astype(BF16)
-    frames_out[...] = wide
+    frames_mine[...] = wide
     wide = wide.astype(F32)
     inverse = lax.rsqrt(jnp.mean(wide * wide, axis=1, keepdims=True) + 1e-05)
     gath[linear] = (latent.astype(F32) * inverse).astype(BF16)
@@ -192,6 +234,10 @@
         for i in range(n_z):
             slot = ((seq + n_seq - j) % n_seq) * n_mp + ((z + n_z - i) % n_z) * 2 + 1 - core
             arrived(slot)
+
+    weight_swaps[1].wait_recv()
+    passed = swap(2, out_pair.at[core], out_pair.at[core], (seq, twin))
+    passed.start()
 
     length = n_mp * frames
     w_q = (folded[0] * HD ** (-0.5)).astype(BF16)
@@ -236,14 +282,121 @@
 
     lax.fori_loop(0, seq, earlier, 0)
     for head in range(heads):
-        attn_out[:, head * HD : (head + 1) * HD] = (accum[head] / total[head]).astype(BF16)
+        at = slice(head * HD, (head + 1) * HD)
+        mixed = (accum[head] / total[head]).astype(BF16).reshape(n_z, 2, frames, HD)
+        for side in range(2):
+            attn_own[side, :, :, at] = mixed[:, side]
+
+    attn_swaps = [swap(3, attn_own.at[1 - core], attn_twin, (seq, twin))]
+    for side in range(2):
+        attn_swaps.append(
+            pltpu.make_async_remote_copy(
+                src_ref=attn_own.at[side],
+                dst_ref=attn_pair.at[core],
+                send_sem=swap_send.at[4 + side],
+                recv_sem=swap_recv.at[4 + core],
+                device_id=(seq, pair * 2 + side),
+                device_id_type=MESH,
+            )
+        )
+    for copy in attn_swaps:
+        copy.start()
+    loads[5].wait()
+    weight_swaps[0].wait_recv()
+    passed.wait_recv()
+    attn_swaps[0].wait_recv()
+
+    chunks = leaving.shape[1]
+    width = leaving.shape[3]
+    plain = chunks - paired_width // width
+
+    def partial(dest, chunk):
+        at = slice(chunk * width, (chunk + 1) * width)
+        value = dot(attn_own[core, dest], out_own[:, at]) + dot(attn_twin[dest], out_twin[:, at])
+        if chunk >= plain:
+            at = slice((chunk - plain) * width, (chunk - plain + 1) * width)
+            for side in range(2):
+                value = value + dot(attn_pair[side, dest], out_pair[side, :, at])
+        return value
+
+    def hop(way, dest, chunk, device):
+        return pltpu.make_async_remote_copy(
+            src_ref=leaving.at[dest, chunk],
+            dst_ref=coming.at[way, dest, chunk],
+            send_sem=chain_send.at[dest, chunk],
+            recv_sem=chain_recv.at[way, dest, chunk],
+            device_id=(seq, device * 2 + core),
+            device_id_type=MESH,
+        )
+
+    def plan(way, dest, chunk):
+        odd = z % 2 == 1
+        if way == 0:
+            if chunk < plain:
+                return z < dest, z > 0, jnp.minimum(z + 1, n_z - 1)
+            return jnp.logical_and(z < dest, odd), z >= 2, jnp.minimum(z + 2, dest)
+        if chunk < plain:
+            return z > dest, z < n_z - 1, jnp.maximum(z - 1, 0)
+        return (
+            jnp.logical_and(z > dest, jnp.logical_not(odd)),
+            z < n_z - 2,
+            jnp.maximum(z - 2, dest),
+        )
+
+    order = [(k, chunk) for k in range(1, n_z) for chunk in range(chunks)]
+    for k, chunk in order:
+        if k == 1 and chunk == plain:
+            for side in range(2):
+                swap(4 + side, attn_own.at[0], attn_pair.at[side], pair_same).wait_recv()
+        for way, dest in ((0, n_z - k), (1, k - 1)):
+            active, has, device = plan(way, dest, chunk)
+
+            @pl.when(active)
+            def _(way=way, dest=dest, chunk=chunk, has=has, device=device):
+                value = partial(dest, chunk)
+
+                @pl.when(has)
+                def _():
+                    hop(way, dest, chunk, pair).wait_recv()
+                    leaving[dest, chunk] = (
+                        value + coming[way, dest, chunk].astype(F32)
+                    ).astype(BF16)
+
+                @pl.when(jnp.logical_not(has))
+                def _():
+                    leaving[dest, chunk] = value.astype(BF16)
+
+                hop(way, dest, chunk, device).start()
+
+    for chunk in range(chunks):
+        at = slice(chunk * width, (chunk + 1) * width)
+        accum_out = frames_mine[:, at].astype(F32) + partial(z, chunk)
+        frames_sum[:, at] = accum_out
+    for chunk in range(chunks):
+        at = slice(chunk * width, (chunk + 1) * width)
+        edges = (z > 0, z < n_z - 1) if chunk < plain else (z >= 2, z < n_z - 2)
+        for way in range(2):
+
+            @pl.when(edges[way])
+            def _(way=way, chunk=chunk, at=at):
+                hop(way, z, chunk, pair).wait_recv()
+                frames_sum[:, at] += coming[way, z, chunk].astype(F32)
+
+        result[:, at] = frames_sum[:, at].astype(BF16)
 
     edge.wait_send()
-    for copy in sent:
+    for copy in sent + weight_swaps + [passed] + attn_swaps:
         copy.wait_send()
-
-
-def front(n_seq, n_mp, audio, first, second, down, proj, gain, qkv):
+    for k, chunk in order:
+        for way, dest in ((0, n_z - k), (1, k - 1)):
+            active, has, device = plan(way, dest, chunk)
+
+            @pl.when(active)
+            def _(way=way, dest=dest, chunk=chunk, device=device):
+                hop(way, dest, chunk, device).wait_send()
+
+
+def layer(n_seq, n_mp, audio, first, second, down, proj, gain, qkv, out):
     rows, channels = audio.shape
     frames = rows // STRIDE
     width = proj.shape[1]
@@ -255,13 +408,10 @@
     hbm = pl.BlockSpec(memory_space=pl.ANY)
     flops = 2 * channels * width * columns * 3 + 12 * rows * channels * channels
     return pl.pallas_call(
-        functools.partial(front_kernel, n_seq, n_mp),
-        out_shape=(
-            jax.ShapeDtypeStruct((frames, width), BF16),
-            jax.ShapeDtypeStruct((length, columns), BF16),
-        ),
-        in_specs=[vmem, hbm, hbm, hbm, hbm, vmem, hbm],
-        out_specs=(vmem, vmem),
+        functools.partial(layer_kernel, n_seq, n_mp),
+        out_shape=jax.ShapeDtypeStruct((frames, width), BF16),
+        in_specs=[vmem, hbm, hbm, hbm, hbm, vmem, hbm, hbm],
+        out_specs=vmem,
         scratch_shapes=[
             pltpu.VMEM((HALO, channels), BF16),
             pltpu.VMEM(first.shape, BF16),
@@ -275,16 +425,30 @@
             pltpu.VMEM((heads, length, 1), F32),
             pltpu.VMEM((heads, length, 1), F32),
             pltpu.VMEM((heads, length, HD), F32),
-            pltpu.SemaphoreType.DMA((5,)),
+            pltpu.VMEM((frames, width), BF16),
+            pltpu.VMEM((frames, width), F32),
+            pltpu.VMEM(out.shape, BF16),
+            pltpu.VMEM(out.shape, BF16),
+            pltpu.VMEM((2, columns, width // 2), BF16),
+            pltpu.VMEM((2, n_z, frames, columns), BF16),
+            pltpu.VMEM((n_z, frames, columns), BF16),
+            pltpu.VMEM((2, n_z, frames, columns), BF16),
+            pltpu.VMEM((n_z, CHUNKS, frames, width // CHUNKS), BF16),
+            pltpu.VMEM((2, n_z, CHUNKS, frames, width // CHUNKS), BF16),
+            pltpu.SemaphoreType.DMA((6,)),
             pltpu.SemaphoreType.DMA((2,)),
             pltpu.SemaphoreType.DMA((n_seq * n_z, n_seq + n_z)),
             pltpu.SemaphoreType.DMA((n_seq * n_mp,)),
+            pltpu.SemaphoreType.DMA((6,)),
+            pltpu.SemaphoreType.DMA((6,)),
+            pltpu.SemaphoreType.DMA((n_z, CHUNKS)),
+            pltpu.SemaphoreType.DMA((2, n_z, CHUNKS)),
         ],
         compiler_params=pltpu.CompilerParams(
-            collective_id=0, has_side_effects=True, vmem_limit_bytes=56 * 2**20
+            collective_id=0, has_side_effects=True, vmem_limit_bytes=60 * 2**20
         ),
         cost_estimate=pl.CostEstimate(flops=flops, bytes_accessed=24 * 2**20, transcendentals=0),
-    )(audio, first, second, down, proj, gain, qkv)
+    )(audio, first, second, down, proj, gain, qkv, out)
 
 
 def body(
@@ -299,7 +463,7 @@
     qkv_weight,
     out_weight,
 ):
-    frames_mine, attn = front(
+    return layer(
         n_seq,
         n_mp,
         audio_feats,
@@ -309,11 +473,8 @@
         in_proj,
         norm_gain.reshape(1, -1),
         qkv_weight,
+        out_weight,
     )
-    summed = lax.psum_scatter(
-        dot(attn, out_weight).astype(BF16), "mp", scatter_dimension=0, tiled=True
-    ).astype(F32)
-    return (frames_mine.astype(F32) + summed).astype(BF16)
 
 
 def solution(mesh):

time: 115 us -> 104 us (0.904)
  the two profiles are of different devices: /device:TPU:6 before, /device:TPU:22 now
where the time goes in v3:
time: 104 us; the launch traced here: 103 us
  Pallas kernels  102 us (98%)
  local copies, waits for them, and re-layouts  1.87 us (2%)
    pallas_call x1, Pallas kernels, layer(): pl.pallas_call(functools.partial(layer_kernel, n_seq, n_mp), out_shape=ja...  102 us

profile of v3, /device:TPU:22, one launch (start us, length us, event | category | flops | bytes accessed | tf_op | source)
XLA Modules:
  0.0 103.4 jit_solution(12192671026511410796)
XLA Ops:
  0.0 101.5 %shard_map.82 = bf16[64,4096]{1,0:T(8,128)(2,1)} custom-call(bf16[512,512]{1,0:T(8,128)(2,1)} %audio.1, bf16[3,3,512,256]{3,2,1,0:T(8,128)(2,1)} %first_hbm.1, bf16[3,256,512]{2,1,0:T(8,128)(2,1)} %second_hbm.1, bf16[16,512,512]{2,1,0:T(8,128)(2,1)} %down_hbm.1, bf16[512,4096]{1,0:T(8,128)(2,1)} %proj_hbm.1, f32[1,4096]{1,0:T(1,128)} %bitcast.1, ...), custom_call_target="tpu_custom_call" | custom-call | flops 4831838208 | bytes 25165824 | tf_op jit(solution)/shard_map/pallas_call | solution.py:410
  101.5 1.9 %copy.10 = bf16[64,4096]{1,0:T(8,128)(2,1)} copy(bf16[64,4096]{1,0:T(8,128)(2,1)} %shard_map.82) | data formatting | bytes 1048576

commit v4 on v3

--- a/solution.py
+++ b/solution.py
@@ -310,14 +310,18 @@
     width = leaving.shape[3]
     plain = chunks - paired_width // width
 
-    def partial(dest, chunk):
+    def whole(ref):
+        return ref[...].reshape(n_z * frames, columns)
+
+    def multiply(chunk):
         at = slice(chunk * width, (chunk + 1) * width)
-        value = dot(attn_own[core, dest], out_own[:, at]) + dot(attn_twin[dest], out_twin[:, at])
+        value = dot(attn_own[core].reshape(n_z * frames, columns), out_own[:, at])
+        value = value + dot(whole(attn_twin), out_twin[:, at])
         if chunk >= plain:
             at = slice((chunk - plain) * width, (chunk - plain + 1) * width)
             for side in range(2):
-                value = value + dot(attn_pair[side, dest], out_pair[side, :, at])
-        return value
+                value = value + dot(whole(attn_pair.at[side]), out_pair[side, :, at])
+        leaving[:, chunk] = value.astype(BF16).reshape(n_z, frames, width)
 
     def hop(way, dest, chunk, device):
         return pltpu.make_async_remote_copy(
@@ -329,52 +333,48 @@
             device_id_type=MESH,
         )
 
-    def plan(way, dest, chunk):
-        odd = z % 2 == 1
-        if way == 0:
-            if chunk < plain:
-                return z < dest, z > 0, jnp.minimum(z + 1, n_z - 1)
-            return jnp.logical_and(z < dest, odd), z >= 2, jnp.minimum(z + 2, dest)
+    last = n_z - 1
+    odd = z % 2
+    near = jnp.where(z < n_z // 2, 0, 1)
+
+    def plan(phase, k, chunk):
+        way = near if phase == 0 else 1 - near
+        dest = jnp.where(way == 0, n_z - k, k - 1)
+        ahead = jnp.where(way == 0, dest - z, z - dest)
+        passed_by = jnp.where(way == 0, z, last - z)
         if chunk < plain:
-            return z > dest, z < n_z - 1, jnp.maximum(z - 1, 0)
-        return (
-            jnp.logical_and(z > dest, jnp.logical_not(odd)),
-            z < n_z - 2,
-            jnp.maximum(z - 2, dest),
-        )
-
-    order = [(k, chunk) for k in range(1, n_z) for chunk in range(chunks)]
-    for k, chunk in order:
-        if k == 1 and chunk == plain:
-            for side in range(2):
-                swap(4 + side, attn_own.at[0], attn_pair.at[side], pair_same).wait_recv()
-        for way, dest in ((0, n_z - k), (1, k - 1)):
-            active, has, device = plan(way, dest, chunk)
-
-            @pl.when(active)
-            def _(way=way, dest=dest, chunk=chunk, has=has, device=device):
-                value = partial(dest, chunk)
-
-                @pl.when(has)
-                def _():
-                    hop(way, dest, chunk, pair).wait_recv()
-                    leaving[dest, chunk] = (
-                        value + coming[way, dest, chunk].astype(F32)
-                    ).astype(BF16)
-
-                @pl.when(jnp.logical_not(has))
-                def _():
-                    leaving[dest, chunk] = value.astype(BF16)
-
-                hop(way, dest, chunk, device).start()
+            active, has, stride = ahead > 0, passed_by > 0, 1
+        else:
+            inner = jnp.where(way == 0, odd, 1 - odd)
+            active, has = jnp.logical_and(ahead > 0, inner == 1), passed_by >= 2
+            stride = jnp.clip(ahead, 0, 2)
+        device = jnp.clip(jnp.where(way == 0, z + stride, z - stride), 0, last)
+        return way, dest, active, has, device
+
+    order = [(p, k, c) for p in range(2) for k in range(1, n_z) for c in range(chunks)]
+    for phase, k, chunk in order:
+        if phase == 0 and k == 1:
+            if chunk == plain:
+                for side in range(2):
+                    swap(4 + side, attn_own.at[0], attn_pair.at[side], pair_same).wait_recv()
+            multiply(chunk)
+        way, dest, active, has, device = plan(phase, k, chunk)
+
+        @pl.when(jnp.logical_and(active, has))
+        def _(way=way, dest=dest, chunk=chunk):
+            hop(way, dest, chunk, pair).wait_recv()
+            leaving[dest, chunk] = (
+                leaving[dest, chunk].astype(F32) + coming[way, dest, chunk].astype(F32)
+            ).astype(BF16)
+
+        @pl.when(active)
+        def _(way=way, dest=dest, chunk=chunk, device=device):
+            hop(way, dest, chunk, device).start()
 
     for chunk in range(chunks):
         at = slice(chunk * width, (chunk + 1) * width)
-        accum_out = frames_mine[:, at].astype(F32) + partial(z, chunk)
-        frames_sum[:, at] = accum_out
-    for chunk in range(chunks):
-        at = slice(chunk * width, (chunk + 1) * width)
-        edges = (z > 0, z < n_z - 1) if chunk < plain else (z >= 2, z < n_z - 2)
+        frames_sum[:, at] = frames_mine[:, at].astype(F32) + leaving[z, chunk].astype(F32)
+        edges = (z > 0, z < last) if chunk < plain else (z >= 2, z < last - 1)
         for way in range(2):
 
             @pl.when(edges[way])
@@ -387,13 +387,12 @@
     edge.wait_send()
     for copy in sent + weight_swaps + [passed] + attn_swaps:
         copy.wait_send()
-    for k, chunk in order:
-        for way, dest in ((0, n_z - k), (1, k - 1)):
-            active, has, device = plan(way, dest, chunk)
-
-            @pl.when(active)
-            def _(way=way, dest=dest, chunk=chunk, device=device):
-                hop(way, dest, chunk, device).wait_send()
+    for phase, k, chunk in order:
+        way, dest, active, has, device = plan(phase, k, chunk)
+
+        @pl.when(active)
+        def _(way=way, dest=dest, chunk=chunk, device=device):
+            hop(way, dest, chunk, device).wait_send()
 
 
 def layer(n_seq, n_mp, audio, first, second, down, proj, gain, qkv, out):

time: 104 us -> 92.3 us (0.89)
  the two profiles are of different devices: /device:TPU:22 before, /device:TPU:15 now
where the time goes in v4:
time: 92.3 us; the launch traced here: 92.2 us
  Pallas kernels  90.3 us (98%)
  local copies, waits for them, and re-layouts  1.87 us (2%)
    pallas_call x1, Pallas kernels, layer(): pl.pallas_call(functools.partial(layer_kernel, n_seq, n_mp), out_shape=ja...  90.3 us
    unnamed x1, local copies, waits for them, and re-layouts  1.87 us

profile of v4, /device:TPU:15, one launch (start us, length us, event | category | flops | bytes accessed | tf_op | source)
XLA Modules:
  0.0 92.2 jit_solution(8252846157845235075)
XLA Ops:
  0.0 90.3 %shard_map.82 = bf16[64,4096]{1,0:T(8,128)(2,1)} custom-call(bf16[512,512]{1,0:T(8,128)(2,1)} %audio.1, bf16[3,3,512,256]{3,2,1,0:T(8,128)(2,1)} %first_hbm.1, bf16[3,256,512]{2,1,0:T(8,128)(2,1)} %second_hbm.1, bf16[16,512,512]{2,1,0:T(8,128)(2,1)} %down_hbm.1, bf16[512,4096]{1,0:T(8,128)(2,1)} %proj_hbm.1, f32[1,4096]{1,0:T(1,128)} %bitcast.1, ...), custom_call_target="tpu_custom_call" | custom-call | flops 4831838208 | bytes 25165824 | tf_op jit(solution)/shard_map/pallas_call | solution.py:409
  90.3 1.9 %copy.10 = bf16[64,4096]{1,0:T(8,128)(2,1)} copy(bf16[64,4096]{1,0:T(8,128)(2,1)} %shard_map.82) | data formatting | bytes 1048576

commit v5 on v4

--- a/solution.py
+++ b/solution.py
@@ -139,15 +139,22 @@
         )
 
     paired_width = out_pair.shape[2]
-    weight_swaps = [
-        swap(0, out_hbm, out_twin, (seq, twin)),
-        swap(
-            1,
-            out_hbm.at[:, pl.ds(out_hbm.shape[1] - paired_width, paired_width)],
-            out_pair.at[core],
+    part = paired_width // 2
+
+    def weight_part(index):
+        begin = out_hbm.shape[1] - paired_width + index * part
+        return swap(
+            1 + index,
+            out_hbm.at[:, pl.ds(begin, part)],
+            out_pair.at[core, :, pl.ds(index * part, part)],
             pair_same,
-        ),
-    ]
+        )
+
+    def pass_part(index):
+        here = out_pair.at[core, :, pl.ds(index * part, part)]
+        return swap(6 + index, here, here, (seq, twin))
+
+    weight_swaps = [swap(0, out_hbm, out_twin, (seq, twin)), weight_part(0)]
     for copy in weight_swaps:
         copy.start()
     edge.wait_recv()
@@ -225,19 +232,8 @@
         for j in range(1, n_seq):
             begin_send(slot, i, j, seq_peer(j))
         begin_send(slot, i, 0, (seq, twin))
-    for j in range(1, n_seq):
-        for i in range(n_z):
-            slot = ((seq + n_seq - j) % n_seq) * n_mp + ((z + n_z - i) % n_z) * 2 + core
-            arrived(slot)
-            begin_send(slot, j * n_z + i, 0, (seq, twin))
-    for j in range(n_seq):
-        for i in range(n_z):
-            slot = ((seq + n_seq - j) % n_seq) * n_mp + ((z + n_z - i) % n_z) * 2 + 1 - core
-            arrived(slot)
-
-    weight_swaps[1].wait_recv()
-    passed = swap(2, out_pair.at[core], out_pair.at[core], (seq, twin))
-    passed.start()
+    weight_swaps.append(weight_part(1))
+    weight_swaps[2].start()
 
     length = n_mp * frames
     w_q = (folded[0] * HD ** (-0.5)).astype(BF16)
@@ -248,12 +244,11 @@
         at = pl.ds(pl.multiple_of(index * n_mp, n_mp), n_mp)
         return gath[at].reshape(length, channels)
 
-    query = dot(block(seq), w_q).astype(BF16)
     peak[...] = jnp.full_like(peak, -1e30)
     total[...] = jnp.zeros_like(total)
     accum[...] = jnp.zeros_like(accum)
 
-    def attend(index, diagonal):
+    def attend(query, index, diagonal):
         source = block(index)
         keys = dot(source, w_k).astype(BF16)
         values = dot(source, w_v).astype(BF16)
@@ -274,13 +269,29 @@
             total[head] = total[head] * factor + jnp.sum(probs, axis=1, keepdims=True)
             accum[head] = accum[head] * factor + dot(probs.astype(BF16), values[:, at])
 
-    attend(seq, True)
-
-    def earlier(index, carry):
-        attend(index, False)
-        return carry
-
-    lax.fori_loop(0, seq, earlier, 0)
+    passed = []
+    for j in range(n_seq):
+        source_seq = (seq + n_seq - j) % n_seq
+        for i in range(n_z):
+            slot = source_seq * n_mp + ((z + n_z - i) % n_z) * 2 + core
+            if j > 0:
+                arrived(slot)
+                begin_send(slot, j * n_z + i, 0, (seq, twin))
+        for i in range(n_z):
+            arrived(source_seq * n_mp + ((z + n_z - i) % n_z) * 2 + 1 - core)
+        if j < 2:
+            weight_swaps[1 + j].wait_recv()
+            passed.append(pass_part(j))
+            passed[j].start()
+        if j == 0:
+            query = dot(block(seq), w_q).astype(BF16)
+            attend(query, seq, True)
+        else:
+
+            @pl.when(seq >= j)
+            def _(j=j):
+                attend(query, seq - j, False)
+
     for head in range(heads):
         at = slice(head * HD, (head + 1) * HD)
         mixed = (accum[head] / total[head]).astype(BF16).reshape(n_z, 2, frames, HD)
@@ -303,7 +314,8 @@
         copy.start()
     loads[5].wait()
     weight_swaps[0].wait_recv()
-    passed.wait_recv()
+    for copy in passed:
+        copy.wait_recv()
     attn_swaps[0].wait_recv()
 
     chunks = leaving.shape[1]
@@ -351,6 +363,13 @@
         device = jnp.clip(jnp.where(way == 0, z + stride, z - stride), 0, last)
         return way, dest, active, has, device
 
+    def settle(phase, k, chunk):
+        way, dest, active, has, device = plan(phase, k, chunk)
+
+        @pl.when(active)
+        def _():
+            hop(way, dest, chunk, device).wait_send()
+
     order = [(p, k, c) for p in range(2) for k in range(1, n_z) for c in range(chunks)]
     for phase, k, chunk in order:
         if phase == 0 and k == 1:
@@ -359,6 +378,8 @@
                     swap(4 + side, attn_own.at[0], attn_pair.at[side], pair_same).wait_recv()
             multiply(chunk)
         way, dest, active, has, device = plan(phase, k, chunk)
+        if k > 1:
+            settle(phase, k - 1, chunk)
 
         @pl.when(jnp.logical_and(active, has))
         def _(way=way, dest=dest, chunk=chunk):
@@ -385,14 +406,11 @@
         result[:, at] = frames_sum[:, at].astype(BF16)
 
     edge.wait_send()
-    for copy in sent + weight_swaps + [passed] + attn_swaps:
+    for copy in sent + weight_swaps + passed + attn_swaps:
         copy.wait_send()
-    for phase, k, chunk in order:
-        way, dest, active, has, device = plan(phase, k, chunk)
-
-        @pl.when(active)
-        def _(way=way, dest=dest, chunk=chunk, device=device):
-            hop(way, dest, chunk, device).wait_send()
+    for phase in range(2):
+        for chunk in range(chunks):
+            settle(phase, last, chunk)
 
 
 def layer(n_seq, n_mp, audio, first, second, down, proj, gain, qkv, out):
@@ -438,8 +456,8 @@
             pltpu.SemaphoreType.DMA((2,)),
             pltpu.SemaphoreType.DMA((n_seq * n_z, n_seq + n_z)),
             pltpu.SemaphoreType.DMA((n_seq * n_mp,)),
-            pltpu.SemaphoreType.DMA((6,)),
-            pltpu.SemaphoreType.DMA((6,)),
+            pltpu.SemaphoreType.DMA((8,)),
+            pltpu.SemaphoreType.DMA((8,)),
             pltpu.SemaphoreType.DMA((n_z, CHUNKS)),
             pltpu.SemaphoreType.DMA((2, n_z, CHUNKS)),
         ],

time: 92.3 us -> 87.1 us (0.944)
  the two profiles are of different devices: /device:TPU:15 before, /device:TPU:6 now
where the time goes in v5:
time: 87.1 us; the launch traced here: 86.9 us
  Pallas kernels  85 us (98%)
  local copies, waits for them, and re-layouts  1.87 us (2%)
    pallas_call x1, Pallas kernels, layer(): pl.pallas_call(functools.partial(layer_kernel, n_seq, n_mp), out_shape=ja...  85 us
    unnamed x1, local copies, waits for them, and re-layouts  1.87 us

profile of v5, /device:TPU:6, one launch (start us, length us, event | category | flops | bytes accessed | tf_op | source)
XLA Modules:
  0.0 86.9 jit_solution(779993723234664073)
XLA Ops:
  0.0 85.0 %shard_map.82 = bf16[64,4096]{1,0:T(8,128)(2,1)} custom-call(bf16[512,512]{1,0:T(8,128)(2,1)} %audio.1, bf16[3,3,512,256]{3,2,1,0:T(8,128)(2,1)} %first_hbm.1, bf16[3,256,512]{2,1,0:T(8,128)(2,1)} %second_hbm.1, bf16[16,512,512]{2,1,0:T(8,128)(2,1)} %down_hbm.1, bf16[512,4096]{1,0:T(8,128)(2,1)} %proj_hbm.1, f32[1,4096]{1,0:T(1,128)} %bitcast.1, ...), custom_call_target="tpu_custom_call" | custom-call | flops 4831838208 | bytes 25165824 | tf_op jit(solution)/shard_map/pallas_call | solution.py:427
  85.1 1.9 %copy.10 = bf16[64,4096]{1,0:T(8,128)(2,1)} copy(bf16[64,4096]{1,0:T(8,128)(2,1)} %shard_map.82) | data formatting | bytes 1048576

commit v6 on v5

--- a/solution.py
+++ b/solution.py
@@ -157,16 +157,19 @@
     weight_swaps = [swap(0, out_hbm, out_twin, (seq, twin)), weight_part(0)]
     for copy in weight_swaps:
         copy.start()
+    loads[0].wait()
+    ready = elu(audio[...].astype(F32)).astype(BF16)
+    ready = [dot(ready, first[0, tap]) for tap in range(3)]
     edge.wait_recv()
     behind = jnp.where(linear == 0, 0.0, halo[...].astype(F32))
     state = jnp.concatenate([behind, audio[...].astype(F32)], axis=0)
     for unit, dilation in enumerate(DILATIONS):
-        u = elu(state).astype(BF16)
+        u = elu(state[:HALO] if unit == 0 else state).astype(BF16)
+        taps = [dot(u, first[unit, tap]) for tap in range(3)]
         if unit == 0:
-            loads[0].wait()
-        middle = dot(u, first[unit, 2])
-        middle = middle + pltpu.roll(dot(u, first[unit, 1]), dilation, 0)
-        middle = middle + pltpu.roll(dot(u, first[unit, 0]), 2 * dilation, 0)
+            taps = [jnp.concatenate(both, axis=0) for both in zip(taps, ready)]
+        middle = taps[2] + pltpu.roll(taps[1], dilation, 0)
+        middle = middle + pltpu.roll(taps[0], 2 * dilation, 0)
         v = elu(middle).astype(BF16)
         if unit == 0:
             loads[1].wait()
@@ -370,12 +373,14 @@
         def _():
             hop(way, dest, chunk, device).wait_send()
 
-    order = [(p, k, c) for p in range(2) for k in range(1, n_z) for c in range(chunks)]
+    paired_first = list(range(plain, chunks)) + list(range(plain))
+    order = [(p, k, c) for p in range(2) for k in range(1, n_z) for c in paired_first]
+    for chunk in range(plain):
+        multiply(chunk)
+    for side in range(2):
+        swap(4 + side, attn_own.at[0], attn_pair.at[side], pair_same).wait_recv()
     for phase, k, chunk in order:
-        if phase == 0 and k == 1:
-            if chunk == plain:
-                for side in range(2):
-                    swap(4 + side, attn_own.at[0], attn_pair.at[side], pair_same).wait_recv()
+        if phase == 0 and k == 1 and chunk >= plain:
             multiply(chunk)
         way, dest, active, has, device = plan(phase, k, chunk)
         if k > 1:

time: 87.1 us -> 87.9 us (level)
  Pallas kernels: 85 us -> 85.9 us
where the time goes in v6:
time: 87.9 us; the launch traced here: 87.7 us
  Pallas kernels  85.9 us (98%)
  local copies, waits for them, and re-layouts  1.87 us (2%)
    pallas_call x1, Pallas kernels, layer(): pl.pallas_call(functools.partial(layer_kernel, n_seq, n_mp), out_shape=ja...  85.9 us
    unnamed x1, local copies, waits for them, and re-layouts  1.87 us

profile of v6, /device:TPU:6, one launch (start us, length us, event | category | flops | bytes accessed | tf_op | source)
XLA Modules:
  0.0 87.7 jit_solution(8735064043039534403)
XLA Ops:
  0.0 85.9 %shard_map.82 = bf16[64,4096]{1,0:T(8,128)(2,1)} custom-call(bf16[512,512]{1,0:T(8,128)(2,1)} %audio.1, bf16[3,3,512,256]{3,2,1,0:T(8,128)(2,1)} %first_hbm.1, bf16[3,256,512]{2,1,0:T(8,128)(2,1)} %second_hbm.1, bf16[16,512,512]{2,1,0:T(8,128)(2,1)} %down_hbm.1, bf16[512,4096]{1,0:T(8,128)(2,1)} %proj_hbm.1, f32[1,4096]{1,0:T(1,128)} %bitcast.1, ...), custom_call_target="tpu_custom_call" | custom-call | flops 4831838208 | bytes 25165824 | tf_op jit(solution)/shard_map/pallas_call | solution.py:432
  85.9 1.9 %copy.10 = bf16[64,4096]{1,0:T(8,128)(2,1)} copy(bf16[64,4096]{1,0:T(8,128)(2,1)} %shard_map.82) | data formatting | bytes 1048576
